TPU v7x, 512 devices: a whole 4x4x16 slice. The times are simulated.
512 devices in a mesh: grp: 16 (over x, z_hi, core), slab: 32 (over y, z_lo).
Axes of the slice: x: 4, y: 4, z: 16 (z_hi: 2, z_lo: 8; z = z_hi * 8 + z_lo), core: 2. Of those that a mesh axis runs over, the one named last changes fastest.
Arguments:
- orbitals: bfloat16 [512, 32768], P(('grp', 'slab')), may hold values from -6 to 6
- offsets: int32 [512, 3], replicated, may hold values from 0 to 8
- slot_pairs: int32 [3072, 2], P(('grp', 'slab')), may hold values from -1 to 511, as said below
Outputs:
- exchange_field: float32 [512, 32768], P(('grp', 'slab'))
- gram: float32 [16, 32, 32], P('grp', None, 'slab')
Inputs may be any that keep to these rules, and one draw needn't show every extreme that they name: `slot_pairs`: rows 6 * d to 6 * d + 5 are the slots of device d (grp index times 32 plus slab index). A slot holds two orbital ids i != j, or -1 in both columns when empty. i lies in the slot's group (id // 32); j in the same group or in the next one (group indices wrap). Each group has exactly 160 filled slots, and some device of each group has all 6 slots filled.
All inputs are finite; a program needn't handle non-finite values.
Results may differ from a plain program's by a relative error of at most 0.0003.
Values may be sent and summed in bfloat16 or wider, within the bound.
A program may use at most 64 MiB of HBM per device.

v0:
```python
import functools
import math
import jax
import jax.numpy as jnp
from jax import lax
from jax.sharding import PartitionSpec as P

SIDE = 32
SHIFT = 8
CHEB = 6
stencil_terms = ((1, 1.5), (2, -0.15), (3, 1.0 / 90.0))
center_term = -49.0 / 18.0


def passed_along(block, axis, distance):
    devices = range(lax.axis_size(axis))
    route = [((i - distance) % len(devices), i) for i in devices]
    return lax.ppermute(block, axis, route)


def sent_together(arrays, axis, dim, along):
    ends, at = ([], 0)
    for a in arrays[:-1]:
        at += a.shape[along]
        ends.append(at)
    both = jnp.concatenate(arrays, axis=along)
    return tuple(jnp.split(lax.all_gather(both, axis, axis=dim, tiled=True), ends, axis=along))


def from_everyone(value, axis):
    size = lax.axis_size(axis)
    return lax.all_to_all(
        jnp.broadcast_to(value[None], (size, *value.shape)), axis, 0, 0, tiled=True
    )


def laid_out(blocks, dim):
    shape = list(blocks.shape[1:])
    shape[dim] *= blocks.shape[0]
    return jnp.moveaxis(blocks, 0, dim).reshape(shape)


def gather_directly(value, axis, dim):
    blocks = from_everyone(value, axis)
    return laid_out(blocks, dim)


def in_blocks(value, dim, size):
    before, after = (value.shape[:dim], value.shape[dim + 1 :])
    return jnp.moveaxis(value.reshape(*before, size, -1, *after), dim, 0)


def edges_of(length, count):
    unit = 8 if length >= 8 * count else 1
    return [length // unit * k // count * unit for k in range(1, count)]


def exchange_in_pieces(value, axis, pieces, split_dim, concat_dim):
    blocks = in_blocks(value, split_dim, lax.axis_size(axis))
    cut = max(range(1, max(2, blocks.ndim - 1)), key=lambda d: blocks.shape[d])
    finished = []
    for piece in jnp.split(blocks, edges_of(blocks.shape[cut], pieces), axis=cut):
        if piece.size:
            finished.append(lax.all_to_all(piece, axis, split_axis=0, concat_axis=0, tiled=True))
    return laid_out(jnp.concatenate(finished, axis=cut), concat_dim)


def summed_on_arrival(value, axis, dim):
    size = lax.axis_size(axis)
    blocks = lax.all_to_all(in_blocks(value, dim, size), axis, 0, 0, tiled=True)
    return jnp.sum(blocks, axis=0)


def slide_cells(values, offset, dim_index):
    extent = values.shape[dim_index]
    pad_shape = list(values.shape)
    pad_shape[dim_index] = abs(offset)
    zero_part = jnp.zeros(pad_shape, values.dtype)
    if offset > 0:
        kept_part = lax.slice_in_dim(values, offset, extent, axis=dim_index)
        return jnp.concatenate((kept_part, zero_part), dim_index)
    kept_part = lax.slice_in_dim(values, 0, extent + offset, axis=dim_index)
    return jnp.concatenate((zero_part, kept_part), dim_index)


def operator(values, box_edge):
    outer_dim = values.ndim - 2
    inner_dim = values.ndim - 1
    zcoord = lax.broadcasted_iota(jnp.int32, (box_edge * box_edge,), 0) % box_edge
    stencil_sum = 3.0 * center_term * values
    for offset, weight in stencil_terms:
        beside = slide_cells(values, offset, outer_dim) + slide_cells(values, -offset, outer_dim)
        beside = (
            beside
            + slide_cells(values, offset * box_edge, inner_dim)
            + slide_cells(values, -offset * box_edge, inner_dim)
        )
        upper_part = jnp.where(
            zcoord + offset < box_edge, slide_cells(values, offset, inner_dim), 0.0
        )
        lower_part = jnp.where(zcoord - offset >= 0, slide_cells(values, -offset, inner_dim), 0.0)
        stencil_sum = stencil_sum + weight * (beside + upper_part + lower_part)
    return -stencil_sum


def coefficients(box_edge, sweeps):
    lowest = 3.0 * (math.pi / (box_edge + 1)) ** 2
    highest = 18.2
    center_value = 0.5 * (highest + lowest)
    half_width = 0.5 * (highest - lowest)
    alpha_list = [1.0 / center_value]
    beta_list = [0.0]
    for step_index in range(1, sweeps):
        previous = alpha_list[-1]
        if step_index == 1:
            beta_now = 0.5 * (half_width * previous) ** 2
        else:
            beta_now = (0.5 * half_width * previous) ** 2
        alpha_list.append(1.0 / (center_value - beta_now / previous))
        beta_list.append(beta_now)
    return (alpha_list, beta_list)


def chebyshev_solve(density, box_edge, sweeps):
    alpha_list, beta_list = coefficients(box_edge, sweeps)
    alpha_table = jnp.asarray(alpha_list, jnp.float32)
    beta_table = jnp.asarray(beta_list, jnp.float32)

    def advance(step_index, state):
        solution, residual, search = state
        search = residual + beta_table[step_index] * search
        solution = solution + alpha_table[step_index] * search
        residual = residual - alpha_table[step_index] * operator(search, box_edge)
        return (solution, residual, search)

    start = (jnp.zeros_like(density), density, jnp.zeros_like(density))
    return lax.fori_loop(0, sweeps, advance, start)[0]


def place_box(box, offset_gap, box_edge, margin):
    cube = box.reshape(box_edge, box_edge, box_edge)
    padded = jnp.pad(cube, margin)
    start = margin - offset_gap
    moved = lax.dynamic_slice(
        padded, (start[0], start[1], start[2]), (box_edge, box_edge, box_edge)
    )
    return moved.reshape(box_edge, box_edge * box_edge)


def on_device(orbitals, offsets, slot_pairs):
    box_edge = SIDE
    cell_count = orbitals.shape[1]
    shaped = functools.partial(place_box, box_edge=box_edge, margin=SHIFT)
    members = lax.axis_size("slab")
    group_count = lax.axis_size("grp")
    group_index = lax.axis_index("grp")
    member_index = lax.axis_index("slab")
    next_box = passed_along(orbitals, "grp", -1)
    near_boxes, far_boxes = sent_together((orbitals, next_box), "slab", 0, 1)
    listing = gather_directly(slot_pairs, "slab", 0)
    live_flags = listing[:, 0] >= 0
    live_ranks = jnp.cumsum(live_flags.astype(jnp.int32)) - 1
    slot_quota = -(-(5 * members) // members)
    targets = member_index * slot_quota + jnp.arange(slot_quota, dtype=jnp.int32)
    select = live_flags[None, :] & (live_ranks[None, :] == targets[:, None])
    chosen_pairs = jnp.sum(jnp.where(select[:, :, None], listing[None, :, :], 0), axis=1)
    live_slot = jnp.any(select, axis=1)
    first_id = group_index * members
    second_id = (group_index + 1) % group_count * members
    own_id = first_id + member_index
    left_id = jnp.where(live_slot, chosen_pairs[:, 0], own_id)
    right_id = jnp.where(live_slot, chosen_pairs[:, 1], own_id)
    left_row = left_id - first_id
    right_row = jnp.where(
        right_id // members == group_index, right_id - first_id, members + right_id - second_id
    )
    box_table = jnp.concatenate((near_boxes, far_boxes), 0)
    offset_gap = offsets[right_id] - offsets[left_id]
    left_box = box_table[left_row].reshape(-1, box_edge, box_edge * box_edge).astype(jnp.float32)
    right_box = jax.vmap(shaped)(box_table[right_row], offset_gap).astype(jnp.float32)
    density = left_box * right_box * live_slot.astype(jnp.float32)[:, None, None]
    potential = chebyshev_solve(density, box_edge, CHEB)
    to_left = (potential * right_box).reshape(-1, cell_count)
    to_right = jax.vmap(shaped)(potential * left_box, -offset_gap).reshape(-1, cell_count)
    partial_fields = jnp.zeros((2 * members, cell_count), jnp.float32)
    partial_fields = partial_fields.at[left_row].add(to_left).at[right_row].add(to_right)
    incoming = passed_along(partial_fields[members:], "grp", 1)
    merged = exchange_in_pieces(partial_fields[:members] + incoming, "slab", 2, 0, 0)
    exchange_field = jnp.sum(merged, 0, keepdims=True)
    anchor = offsets[first_id]
    own_shift = offsets[own_id] - anchor
    framed_field = shaped(exchange_field[0], own_shift).astype(jnp.bfloat16).reshape(1, cell_count)
    norm_factor = 1.0 / math.sqrt(cell_count)
    framed_orbital = shaped(orbitals[0], own_shift).reshape(1, cell_count)
    orbital_slabs, field_slabs = (
        lax.all_to_all(framed_orbital, "slab", split_axis=1, concat_axis=0, tiled=True),
        lax.all_to_all(framed_field, "slab", split_axis=1, concat_axis=0, tiled=True),
    )
    partial_gram = (
        lax.dot_general(
            orbital_slabs, field_slabs, (((1,), (1,)), ((), ())), preferred_element_type=jnp.float32
        )
        * norm_factor
    )
    column = summed_on_arrival(partial_gram, "slab", 1)
    gram_block = column.reshape(1, members, 1)
    return (exchange_field, gram_block)


def solution(mesh):
    return jax.shard_map(
        on_device,
        mesh=mesh,
        in_specs=(P(("grp", "slab"), None), P(), P(("grp", "slab"), None)),
        out_specs=(P(("grp", "slab"), None), P("grp", None, "slab")),
        check_vma=False,
    )
```

profile of v0, /device:TPU:2, one launch (start us, length us, event | category | flops | bytes accessed | tf_op | source)
XLA Modules:
  0.0 873.7 jit_solution(8631526173494886654)
XLA Ops:
  7.2 15.1 %collective-permute-start = (bf16[1,32768]{1,0:T(2,128)(2,1)}, bf16[1,32768]{1,0:T(2,128)(2,1)S(1)}, u32[]{:S(2)}, u32[]{:S(2)}) collective-permute-start(bf16[1,32768]{1,0:T(2,128)(2,1)} %param.7), channel_id=1, source_target_pairs={{32,0},{64,32},{96,64},{128,96},{160,128},{192,160},{224,192},{256... | collective-permute-start | bytes 196616 | tf_op jit(solution)/shard_map/ppermute | solution.py:18
  28.7 9.3 %all-to-all-start = ((s32[32,6,2]{1,2,0:T(2,128)}), s32[32,6,2]{1,2,0:T(2,128)S(1)}, u32[]{:S(2)}, u32[]{:S(2)}) async-start(s32[32,6,2]{1,2,0:T(2,128)} %broadcast_in_dim.132), calls=%async_computation | async-start | bytes 65536 | tf_op jit(solution)/shard_map/all_to_all | solution.py:32
  38.9 11.6 %all-to-all-done = s32[32,6,2]{1,2,0:T(2,128)S(1)} async-done(((s32[32,6,2]{1,2,0:T(2,128)}), s32[32,6,2]{1,2,0:T(2,128)S(1)}, u32[]{:S(2)}, u32[]{:S(2)}) %all-to-all-start) | async-done | bytes 1568 | tf_op jit(solution)/shard_map/all_to_all | solution.py:32
  53.4 237.7 %all-gather.3.cloned.1.call-done = bf16[32,1,65536]{2,1,0:T(2,128)(2,1)} async-done(((bf16[1,1,65536]{2,1,0:T(2,128)(2,1)}), bf16[32,1,65536]{2,1,0:T(2,128)(2,1)}) %all-gather.3.cloned.1.call-update) | async-done | bytes 4194320 | tf_op jit(solution)/shard_map/all_gather | solution.py:27
  291.1 8.0 copy.77
  301.6 3.8 gather_fusion.1
  308.6 25.1 %while.23 = (s32[]{:T(128)}, bf16[5,48,48,48]{3,2,1,0:T(8,128)(2,1)}, s32[5,4]{1,0:T(8,128)S(1)}, bf16[5,32,32,32]{3,2,1,0:T(8,128)(2,1)}, s32[]{:T(128)}) while((s32[]{:T(128)}, bf16[5,48,48,48]{3,2,1,0:T(8,128)(2,1)}, s32[5,4]{1,0:T(8,128)S(1)}, bf16[5,32,32,32]{3,2,1,0:T(8,128)(2,1)}, s32[]{:T(128)}) %tuple.145), condition=%wide.while_cond, body=%wide.while_body.sunk | while | flops 2 | bytes 526977 | solution.py:144
  309.2 4.4 dynamic-slice_dynamic-update-slice_fusion.4
  314.3 4.4 dynamic-slice_dynamic-update-slice_fusion.4
  319.3 4.4 dynamic-slice_dynamic-update-slice_fusion.4
  324.3 4.3 dynamic-slice_dynamic-update-slice_fusion.4
  329.3 4.4 dynamic-slice_dynamic-update-slice_fusion.4
  336.9 3.8 gather_fusion
  342.4 42.8 %while.25 = (s32[]{:T(128)}, f32[5,32,1024]{2,1,0:T(8,128)S(1)}, f32[5,32,1024]{2,1,0:T(8,128)S(1)}, f32[5,32,1024]{2,1,0:T(8,128)S(1)}, s32[]{:T(128)}, /*index=5*/f32[6]{0:T(128)S(1)}, s32[]{:T(128)}, f32[6]{0:T(128)S(1)}) while((s32[]{:T(128)}, f32[5,32,1024]{2,1,0:T(8,128)S(1)}, f32[5,32,1024]{2,1,0:T(8,128)S(1)}, ...), condition=%wide.region_5.6_spmd.clone.clone, body=%wide.region_4.5_spmd.sunk.clone.clone.sunk | while | flops 6092803 | bytes 39147136 | solution.py:137
  393.3 26.0 %while.24 = (s32[]{:T(128)}, f32[5,48,48,48]{3,2,1,0:T(8,128)}, s32[5,4]{1,0:T(8,128)S(1)}, f32[5,32,32,32]{3,2,1,0:T(8,128)}, s32[]{:T(128)}) while((s32[]{:T(128)}, f32[5,48,48,48]{3,2,1,0:T(8,128)}, s32[5,4]{1,0:T(8,128)S(1)}, f32[5,32,32,32]{3,2,1,0:T(8,128)}, s32[]{:T(128)}) %tuple.151), condition=%wide.while_cond.1, body=%wide.while_body.1.sunk | while | flops 2 | bytes 1051265 | solution.py:144
  393.9 4.6 dynamic-slice_dynamic-update-slice_fusion.5
  399.1 4.6 dynamic-slice_dynamic-update-slice_fusion.5
  404.4 4.6 dynamic-slice_dynamic-update-slice_fusion.5
  409.5 4.6 dynamic-slice_dynamic-update-slice_fusion.5
  414.7 4.6 dynamic-slice_dynamic-update-slice_fusion.5
  422.5 5.0 scatter_custom_fusion
  427.5 8.1 scatter_fusion
  440.4 114.9 %collective-permute-done.1 = f32[32,32768]{1,0:T(8,128)S(1)} collective-permute-done((f32[32,32768]{1,0:T(8,128)S(1)}, f32[32,32768]{1,0:T(8,128)S(1)}, u32[]{:S(2)}, u32[]{:S(2)}) %collective-permute-start.1) | collective-permute-done | bytes 4194336 | tf_op jit(solution)/shard_map/ppermute | solution.py:18
  555.8 4.0 reshape.153
  559.8 71.3 %all-to-all-start.1 = ((f32[32,1,32768]{2,1,0:T(1,128)}), f32[32,1,32768]{2,1,0:T(1,128)}, u32[]{:S(2)}, u32[]{:S(2)}) async-start(f32[32,1,32768]{2,1,0:T(1,128)} %reshape.153), calls=%async_computation.1 | async-start | bytes 8388608 | tf_op jit(solution)/shard_map/all_to_all | solution.py:64
  640.7 162.0 %all-to-all-done.1 = f32[32,1,32768]{2,1,0:T(1,128)} async-done(((f32[32,1,32768]{2,1,0:T(1,128)}), f32[32,1,32768]{2,1,0:T(1,128)}, u32[]{:S(2)}, u32[]{:S(2)}) %all-to-all-start.1) | async-done | bytes 4194336 | tf_op jit(solution)/shard_map/all_to_all | solution.py:64
  802.8 14.4 %all-to-all-start.2 = ((bf16[32,2,512]{2,1,0:T(2,128)(2,1)}), bf16[32,2,512]{2,1,0:T(2,128)(2,1)S(1)}, u32[]{:S(2)}, u32[]{:S(2)}) async-start(bf16[32,2,512]{2,1,0:T(2,128)(2,1)} %reshape.274), calls=%async_computation.2 | async-start | bytes 131072 | tf_op jit(solution)/shard_map/all_to_all | solution.py:196
  817.2 4.9 reduce_sum.28
  824.6 5.2 all-to-all-done.2
  829.8 7.3 all-to-all-start.3
  837.2 12.6 %all-to-all-done.3 = bf16[32,2,512]{2,1,0:T(2,128)(2,1)S(1)} async-done(((bf16[32,2,512]{2,1,0:T(2,128)(2,1)}), bf16[32,2,512]{2,1,0:T(2,128)(2,1)S(1)}, u32[]{:S(2)}, u32[]{:S(2)}) %all-to-all-start.3) | async-done | bytes 65568 | tf_op jit(solution)/shard_map/all_to_all | solution.py:197
  850.0 16.2 %all_to_all.45 = f32[32,32,1]{1,2,0:T(1,128)S(1)} all-to-all(f32[32,32,1]{1,2,0:T(1,128)S(1)} %copy.50), channel_id=1, replica_groups=mesh['grp'=16,'slab'=32] {'slab'}, dimensions={0} | all-to-all | bytes 8192 | tf_op jit(solution)/shard_map/all_to_all | solution.py:70
  (199 shorter events, 93.2 us)
Async XLA Ops:
  7.2 284.0 %all-gather.3.cloned.1.call-start = ((), (), s32[]{:S(2)}) async-start(), calls=%async_computation.5 | async-start | bytes 8650752 | tf_op jit(solution)/shard_map/all_gather | solution.py:27
  7.2 18.3 %collective-permute-start = (bf16[1,32768]{1,0:T(2,128)(2,1)}, bf16[1,32768]{1,0:T(2,128)(2,1)S(1)}, u32[]{:S(2)}, u32[]{:S(2)}) collective-permute-start(bf16[1,32768]{1,0:T(2,128)(2,1)} %param.7), channel_id=1, source_target_pairs={{32,0},{64,32},{96,64},{128,96},{160,128},{192,160},{224,192},{256... | collective-permute-start | bytes 196616 | tf_op jit(solution)/shard_map/ppermute | solution.py:18
  28.7 21.8 %all-to-all-start = ((s32[32,6,2]{1,2,0:T(2,128)}), s32[32,6,2]{1,2,0:T(2,128)S(1)}, u32[]{:S(2)}, u32[]{:S(2)}) async-start(s32[32,6,2]{1,2,0:T(2,128)} %broadcast_in_dim.132), calls=%async_computation | async-start | bytes 65536 | tf_op jit(solution)/shard_map/all_to_all | solution.py:32
  336.9 5.4 copy-start.5
  336.9 5.4 copy-start.6
  393.3 28.8 %copy-start.1 = (f32[1,5,32,1024]{3,2,1,0:T(8,128)S(1)}, f32[1,5,32,1024]{3,2,1,0:T(8,128)}, u32[]{:S(2)}) copy-start(f32[1,5,32,1024]{3,2,1,0:T(8,128)} %get-tuple-element.316) | copy-start | bytes 1966084
  435.6 119.8 %copy-start = (f32[64,32768]{1,0:T(8,128)S(1)}, f32[64,32768]{1,0:T(8,128)}, u32[]{:S(2)}) copy-start(f32[64,32768]{1,0:T(8,128)} %scatter_fusion) | copy-start | bytes 25165828
  438.2 117.1 %collective-permute-start.1 = (f32[32,32768]{1,0:T(8,128)S(1)}, f32[32,32768]{1,0:T(8,128)S(1)}, u32[]{:S(2)}, u32[]{:S(2)}) collective-permute-start(f32[32,32768]{1,0:T(8,128)S(1)} %slice.373), channel_id=1, source_target_pairs={{480,0},{0,32},{32,64},{64,96},{96,128},{128,160},{160,192},{192,2... | collective-permute-start | bytes 12582920 | tf_op jit(solution)/shard_map/ppermute | solution.py:18
  559.8 71.4 %copy-start.4 = (s32[512,3]{0,1:T(4,128)S(1)}, s32[512,3]{0,1:T(4,128)}, u32[]{:S(2)}) copy-start(s32[512,3]{0,1:T(4,128)} %param.8) | copy-start | bytes 18436
  559.8 75.7 %copy-start.3 = (bf16[1,32768]{1,0:T(2,128)(2,1)S(1)}, bf16[1,32768]{1,0:T(2,128)(2,1)}, u32[]{:S(2)}) copy-start(bf16[1,32768]{1,0:T(2,128)(2,1)} %param.7) | copy-start | bytes 196612
  559.8 243.0 %all-to-all-start.1 = ((f32[32,1,32768]{2,1,0:T(1,128)}), f32[32,1,32768]{2,1,0:T(1,128)}, u32[]{:S(2)}, u32[]{:S(2)}) async-start(f32[32,1,32768]{2,1,0:T(1,128)} %reshape.153), calls=%async_computation.1 | async-start | bytes 8388608 | tf_op jit(solution)/shard_map/all_to_all | solution.py:64
  802.8 27.0 %all-to-all-start.2 = ((bf16[32,2,512]{2,1,0:T(2,128)(2,1)}), bf16[32,2,512]{2,1,0:T(2,128)(2,1)S(1)}, u32[]{:S(2)}, u32[]{:S(2)}) async-start(bf16[32,2,512]{2,1,0:T(2,128)(2,1)} %reshape.274), calls=%async_computation.2 | async-start | bytes 131072 | tf_op jit(solution)/shard_map/all_to_all | solution.py:196
  822.1 44.7 %copy-start.2 = (f32[32768]{0:T(1024)}, f32[32768]{0:T(1024)S(1)}, u32[]{:S(2)}) copy-start(f32[32768]{0:T(1024)S(1)} %reduce_sum.28) | copy-start | bytes 393220
  829.8 20.0 %all-to-all-start.3 = ((bf16[32,2,512]{2,1,0:T(2,128)(2,1)}), bf16[32,2,512]{2,1,0:T(2,128)(2,1)S(1)}, u32[]{:S(2)}, u32[]{:S(2)}) async-start(bf16[32,2,512]{2,1,0:T(2,128)(2,1)} %reshape.272), calls=%async_computation.3 | async-start | bytes 131072 | tf_op jit(solution)/shard_map/all_to_all | solution.py:197
Sparse Core Ops, SparseCore 0:
  27.5 263.5 all-gather.2
where the time goes:
time: 875 us; the launch traced here: 874 us
  waiting for transfers between devices  547 us (63%)
  starting transfers between devices  120 us (14%)
  local copies, waits for them, and re-layouts  114 us (13%)
  other arithmetic  55.6 us (6%)
  between operations  20 us (2%)
  blocking collectives  16.2 us (2%)
    all_gather x1, waiting for transfers between devices, sent_together(): lax.all_gather(both, axis, axis=dim, tiled=True)  238 us
    all_to_all x1, waiting for transfers between devices, exchange_in_pieces(): lax.all_to_all(piece, axis, split_axis=0, concat_axis=0, tiled=True)  162 us
    ppermute x2, waiting for transfers between devices, passed_along(): return lax.ppermute(block, axis, route)  118 us
    all_to_all x1, starting transfers between devices, exchange_in_pieces(): lax.all_to_all(piece, axis, split_axis=0, concat_axis=0, tiled=True)  71.3 us
    gather x30, local copies, waits for them, and re-layouts  51 us
  transfers between devices with their start and end apart: 7, of which 7 were waited for; matrix products, arithmetic and copies ran while one was open for 2% of the time, Pallas kernels for 0%

commit v1 on v0

--- a/solution.py
+++ b/solution.py
@@ -194,7 +194,12 @@
     framed_orbital = shaped(orbitals[0], own_shift).reshape(1, cell_count)
     orbital_slabs, field_slabs = (
         lax.all_to_all(framed_orbital, "slab", split_axis=1, concat_axis=0, tiled=True),
-        lax.all_to_all(framed_field, "slab", split_axis=1, concat_axis=0, tiled=True),
+        jnp.concatenate(
+            lax.all_to_all(
+                jnp.stack(jnp.split(framed_field, lax.axis_size("slab"), axis=1)), "slab", 0, 0
+            ),
+            axis=0,
+        ),
     )
     partial_gram = (
         lax.dot_general(

time: 875 us -> 876 us (level)
  no operation moved by 1% of the time
where the time goes in v1:
time: 876 us; the launch traced here: 874 us
  waiting for transfers between devices  547 us (62%)
  starting transfers between devices  120 us (14%)
  local copies, waits for them, and re-layouts  115 us (13%)
  other arithmetic  55.6 us (6%)
  between operations  20.1 us (2%)
  blocking collectives  16.2 us (2%)
    all_gather x1, waiting for transfers between devices, sent_together(): lax.all_gather(both, axis, axis=dim, tiled=True)  238 us
    all_to_all x1, waiting for transfers between devices, exchange_in_pieces(): lax.all_to_all(piece, axis, split_axis=0, concat_axis=0, tiled=True)  162 us
    ppermute x2, waiting for transfers between devices, passed_along(): return lax.ppermute(block, axis, route)  118 us
    all_to_all x1, starting transfers between devices, exchange_in_pieces(): lax.all_to_all(piece, axis, split_axis=0, concat_axis=0, tiled=True)  71.3 us
    gather x30, local copies, waits for them, and re-layouts  51 us
  transfers between devices with their start and end apart: 7, of which 7 were waited for; matrix products, arithmetic and copies ran while one was open for 2% of the time, Pallas kernels for 0%

profile of v1, /device:TPU:2, one launch (start us, length us, event | category | flops | bytes accessed | tf_op | source)
XLA Modules:
  0.0 874.2 jit_solution(18266301814595298100)
XLA Ops:
  7.2 15.1 %collective-permute-start = (bf16[1,32768]{1,0:T(2,128)(2,1)}, bf16[1,32768]{1,0:T(2,128)(2,1)S(1)}, u32[]{:S(2)}, u32[]{:S(2)}) collective-permute-start(bf16[1,32768]{1,0:T(2,128)(2,1)} %param.7), channel_id=1, source_target_pairs={{32,0},{64,32},{96,64},{128,96},{160,128},{192,160},{224,192},{256... | collective-permute-start | bytes 196616 | tf_op jit(solution)/shard_map/ppermute | solution.py:18
  28.7 9.3 %all-to-all-start = ((s32[32,6,2]{1,2,0:T(2,128)}), s32[32,6,2]{1,2,0:T(2,128)S(1)}, u32[]{:S(2)}, u32[]{:S(2)}) async-start(s32[32,6,2]{1,2,0:T(2,128)} %broadcast_in_dim.132), calls=%async_computation | async-start | bytes 65536 | tf_op jit(solution)/shard_map/all_to_all | solution.py:32
  38.9 11.6 %all-to-all-done = s32[32,6,2]{1,2,0:T(2,128)S(1)} async-done(((s32[32,6,2]{1,2,0:T(2,128)}), s32[32,6,2]{1,2,0:T(2,128)S(1)}, u32[]{:S(2)}, u32[]{:S(2)}) %all-to-all-start) | async-done | bytes 1568 | tf_op jit(solution)/shard_map/all_to_all | solution.py:32
  53.4 237.7 %all-gather.3.cloned.1.call-done = bf16[32,1,65536]{2,1,0:T(2,128)(2,1)} async-done(((bf16[1,1,65536]{2,1,0:T(2,128)(2,1)}), bf16[32,1,65536]{2,1,0:T(2,128)(2,1)}) %all-gather.3.cloned.1.call-update) | async-done | bytes 4194320 | tf_op jit(solution)/shard_map/all_gather | solution.py:27
  291.1 8.0 copy.75
  301.6 3.8 gather_fusion.1
  308.6 25.1 %while.23 = (s32[]{:T(128)}, bf16[5,48,48,48]{3,2,1,0:T(8,128)(2,1)}, s32[5,4]{1,0:T(8,128)S(1)}, bf16[5,32,32,32]{3,2,1,0:T(8,128)(2,1)}, s32[]{:T(128)}) while((s32[]{:T(128)}, bf16[5,48,48,48]{3,2,1,0:T(8,128)(2,1)}, s32[5,4]{1,0:T(8,128)S(1)}, bf16[5,32,32,32]{3,2,1,0:T(8,128)(2,1)}, s32[]{:T(128)}) %tuple.145), condition=%wide.while_cond, body=%wide.while_body.sunk | while | flops 2 | bytes 526977 | solution.py:144
  309.2 4.4 dynamic-slice_dynamic-update-slice_fusion.4
  314.3 4.4 dynamic-slice_dynamic-update-slice_fusion.4
  319.3 4.4 dynamic-slice_dynamic-update-slice_fusion.4
  324.3 4.3 dynamic-slice_dynamic-update-slice_fusion.4
  329.3 4.4 dynamic-slice_dynamic-update-slice_fusion.4
  336.9 3.8 gather_fusion
  342.4 42.8 %while.25 = (s32[]{:T(128)}, f32[5,32,1024]{2,1,0:T(8,128)S(1)}, f32[5,32,1024]{2,1,0:T(8,128)S(1)}, f32[5,32,1024]{2,1,0:T(8,128)S(1)}, s32[]{:T(128)}, /*index=5*/f32[6]{0:T(128)S(1)}, s32[]{:T(128)}, f32[6]{0:T(128)S(1)}) while((s32[]{:T(128)}, f32[5,32,1024]{2,1,0:T(8,128)S(1)}, f32[5,32,1024]{2,1,0:T(8,128)S(1)}, ...), condition=%wide.region_5.6_spmd.clone.clone, body=%wide.region_4.5_spmd.sunk.clone.clone.sunk | while | flops 6092803 | bytes 39147136 | solution.py:137
  393.3 26.0 %while.24 = (s32[]{:T(128)}, f32[5,48,48,48]{3,2,1,0:T(8,128)}, s32[5,4]{1,0:T(8,128)S(1)}, f32[5,32,32,32]{3,2,1,0:T(8,128)}, s32[]{:T(128)}) while((s32[]{:T(128)}, f32[5,48,48,48]{3,2,1,0:T(8,128)}, s32[5,4]{1,0:T(8,128)S(1)}, f32[5,32,32,32]{3,2,1,0:T(8,128)}, s32[]{:T(128)}) %tuple.151), condition=%wide.while_cond.1, body=%wide.while_body.1.sunk | while | flops 2 | bytes 1051265 | solution.py:144
  393.9 4.6 dynamic-slice_dynamic-update-slice_fusion.5
  399.1 4.6 dynamic-slice_dynamic-update-slice_fusion.5
  404.4 4.6 dynamic-slice_dynamic-update-slice_fusion.5
  409.5 4.6 dynamic-slice_dynamic-update-slice_fusion.5
  414.7 4.6 dynamic-slice_dynamic-update-slice_fusion.5
  422.5 5.0 scatter_custom_fusion
  427.5 8.1 scatter_fusion
  440.4 114.9 %collective-permute-done.1 = f32[32,32768]{1,0:T(8,128)S(1)} collective-permute-done((f32[32,32768]{1,0:T(8,128)S(1)}, f32[32,32768]{1,0:T(8,128)S(1)}, u32[]{:S(2)}, u32[]{:S(2)}) %collective-permute-start.1) | collective-permute-done | bytes 4194336 | tf_op jit(solution)/shard_map/ppermute | solution.py:18
  555.8 4.0 reshape.149
  559.8 71.3 %all-to-all-start.1 = ((f32[32,1,32768]{2,1,0:T(1,128)}), f32[32,1,32768]{2,1,0:T(1,128)}, u32[]{:S(2)}, u32[]{:S(2)}) async-start(f32[32,1,32768]{2,1,0:T(1,128)} %reshape.149), calls=%async_computation.1 | async-start | bytes 8388608 | tf_op jit(solution)/shard_map/all_to_all | solution.py:64
  640.7 162.0 %all-to-all-done.1 = f32[32,1,32768]{2,1,0:T(1,128)} async-done(((f32[32,1,32768]{2,1,0:T(1,128)}), f32[32,1,32768]{2,1,0:T(1,128)}, u32[]{:S(2)}, u32[]{:S(2)}) %all-to-all-start.1) | async-done | bytes 4194336 | tf_op jit(solution)/shard_map/all_to_all | solution.py:64
  802.8 14.4 %all-to-all-start.2 = ((bf16[32,2,512]{2,1,0:T(2,128)(2,1)}), bf16[32,2,512]{2,1,0:T(2,128)(2,1)S(1)}, u32[]{:S(2)}, u32[]{:S(2)}) async-start(bf16[32,2,512]{2,1,0:T(2,128)(2,1)} %reshape.271), calls=%async_computation.2 | async-start | bytes 131072 | tf_op jit(solution)/shard_map/all_to_all | solution.py:196
  817.2 4.9 reduce_sum.28
  825.1 4.7 all-to-all-done.2
  829.8 7.8 all-to-all-start.3
  837.7 12.6 %all-to-all-done.3 = bf16[32,2,512]{2,1,0:T(2,128)(2,1)S(1)} async-done(((bf16[32,2,512]{2,1,0:T(2,128)(2,1)}), bf16[32,2,512]{2,1,0:T(2,128)(2,1)S(1)}, u32[]{:S(2)}, u32[]{:S(2)}) %all-to-all-start.3) | async-done | bytes 65568 | tf_op jit(solution)/shard_map/all_to_all | solution.py:198
  850.5 16.2 %all_to_all.37 = f32[32,32,1]{1,2,0:T(1,128)S(1)} all-to-all(f32[32,32,1]{1,2,0:T(1,128)S(1)} %copy.48), channel_id=1, replica_groups=mesh['grp'=16,'slab'=32] {'slab'}, dimensions={0} | all-to-all | bytes 8192 | tf_op jit(solution)/shard_map/all_to_all | solution.py:70
  (231 shorter events, 93.6 us)
Async XLA Ops:
  7.2 284.0 %all-gather.3.cloned.1.call-start = ((), (), s32[]{:S(2)}) async-start(), calls=%async_computation.5 | async-start | bytes 8650752 | tf_op jit(solution)/shard_map/all_gather | solution.py:27
  7.2 18.3 %collective-permute-start = (bf16[1,32768]{1,0:T(2,128)(2,1)}, bf16[1,32768]{1,0:T(2,128)(2,1)S(1)}, u32[]{:S(2)}, u32[]{:S(2)}) collective-permute-start(bf16[1,32768]{1,0:T(2,128)(2,1)} %param.7), channel_id=1, source_target_pairs={{32,0},{64,32},{96,64},{128,96},{160,128},{192,160},{224,192},{256... | collective-permute-start | bytes 196616 | tf_op jit(solution)/shard_map/ppermute | solution.py:18
  28.7 21.8 %all-to-all-start = ((s32[32,6,2]{1,2,0:T(2,128)}), s32[32,6,2]{1,2,0:T(2,128)S(1)}, u32[]{:S(2)}, u32[]{:S(2)}) async-start(s32[32,6,2]{1,2,0:T(2,128)} %broadcast_in_dim.132), calls=%async_computation | async-start | bytes 65536 | tf_op jit(solution)/shard_map/all_to_all | solution.py:32
  336.9 5.4 copy-start.5
  336.9 5.4 copy-start.6
  393.3 28.8 %copy-start.1 = (f32[1,5,32,1024]{3,2,1,0:T(8,128)S(1)}, f32[1,5,32,1024]{3,2,1,0:T(8,128)}, u32[]{:S(2)}) copy-start(f32[1,5,32,1024]{3,2,1,0:T(8,128)} %get-tuple-element.316) | copy-start | bytes 1966084
  435.6 119.8 %copy-start = (f32[64,32768]{1,0:T(8,128)S(1)}, f32[64,32768]{1,0:T(8,128)}, u32[]{:S(2)}) copy-start(f32[64,32768]{1,0:T(8,128)} %scatter_fusion) | copy-start | bytes 25165828
  438.2 117.1 %collective-permute-start.1 = (f32[32,32768]{1,0:T(8,128)S(1)}, f32[32,32768]{1,0:T(8,128)S(1)}, u32[]{:S(2)}, u32[]{:S(2)}) collective-permute-start(f32[32,32768]{1,0:T(8,128)S(1)} %slice.373), channel_id=1, source_target_pairs={{480,0},{0,32},{32,64},{64,96},{96,128},{128,160},{160,192},{192,2... | collective-permute-start | bytes 12582920 | tf_op jit(solution)/shard_map/ppermute | solution.py:18
  559.8 71.4 %copy-start.4 = (s32[512,3]{0,1:T(4,128)S(1)}, s32[512,3]{0,1:T(4,128)}, u32[]{:S(2)}) copy-start(s32[512,3]{0,1:T(4,128)} %param.8) | copy-start | bytes 18436
  559.8 75.7 %copy-start.3 = (bf16[1,32768]{1,0:T(2,128)(2,1)S(1)}, bf16[1,32768]{1,0:T(2,128)(2,1)}, u32[]{:S(2)}) copy-start(bf16[1,32768]{1,0:T(2,128)(2,1)} %param.7) | copy-start | bytes 196612
  559.8 243.0 %all-to-all-start.1 = ((f32[32,1,32768]{2,1,0:T(1,128)}), f32[32,1,32768]{2,1,0:T(1,128)}, u32[]{:S(2)}, u32[]{:S(2)}) async-start(f32[32,1,32768]{2,1,0:T(1,128)} %reshape.149), calls=%async_computation.1 | async-start | bytes 8388608 | tf_op jit(solution)/shard_map/all_to_all | solution.py:64
  802.8 27.0 %all-to-all-start.2 = ((bf16[32,2,512]{2,1,0:T(2,128)(2,1)}), bf16[32,2,512]{2,1,0:T(2,128)(2,1)S(1)}, u32[]{:S(2)}, u32[]{:S(2)}) async-start(bf16[32,2,512]{2,1,0:T(2,128)(2,1)} %reshape.271), calls=%async_computation.2 | async-start | bytes 131072 | tf_op jit(solution)/shard_map/all_to_all | solution.py:196
  822.1 45.2 %copy-start.2 = (f32[32768]{0:T(1024)}, f32[32768]{0:T(1024)S(1)}, u32[]{:S(2)}) copy-start(f32[32768]{0:T(1024)S(1)} %reduce_sum.28) | copy-start | bytes 393220
  829.8 20.5 %all-to-all-start.3 = ((bf16[32,2,512]{2,1,0:T(2,128)(2,1)}), bf16[32,2,512]{2,1,0:T(2,128)(2,1)S(1)}, u32[]{:S(2)}, u32[]{:S(2)}) async-start(bf16[32,2,512]{2,1,0:T(2,128)(2,1)} %reshape.269), calls=%async_computation.3 | async-start | bytes 131072 | tf_op jit(solution)/shard_map/all_to_all | solution.py:198
Sparse Core Ops, SparseCore 0:
  27.5 263.5 all-gather.2
